TPU v7x, 32 devices: a whole 2x2x4 slice. The times are simulated.
32 devices in a mesh: pair: 8 (over z, y), sec: 4 (over x, core).
Axes of the slice: x: 2, y: 2, z: 4, core: 2. Of those that a mesh axis runs over, the one named last changes fastest.
Arguments:
- psi: bfloat16 [32, 768, 384], P('sec'), may hold values from -6 to 6
- sec_rows: int32 [32], replicated, may hold values from 128 to 768, as said below
- match: int32 [32], replicated, may hold values from 0 to 31, each once
- normal_ops: bfloat16 [8, 32, 768, 768], P('pair', 'sec'), may hold values from -0.078125 to 0.078125
- comp_ops: bfloat16 [8, 32, 384, 384], P('pair', 'sec'), may hold values from -0.3125 to 0.3125
Outputs:
- sigma: bfloat16 [32, 768, 384], P('sec', 'pair')
Inputs may be any that keep to these rules, and one draw needn't show every extreme that they name: `sec_rows`: every entry is a multiple of 128; some entry equals 768 in every draw.
All inputs are finite; a program needn't handle non-finite values.
Results may differ from a plain program's by a relative error of at most 0.0049.
Values may be sent and summed in bfloat16 or wider, within the bound.
A program may use at most 128 MiB of HBM per device.

v0:
```python
import jax
import jax.numpy as jnp
from jax import lax
from jax.sharding import PartitionSpec as P


def pick_sources(gathered, match, targets):
    total = match.shape[0]
    hits = match[None, :] == targets[:, None]
    source = jnp.sum(jnp.where(hits, jnp.arange(total, dtype=jnp.int32)[None, :], 0), axis=1)
    return gathered[source]


def shards(psi, sec_rows, match, normal_ops, comp_ops):
    sec_dev = psi.shape[0]
    block_rows = psi.shape[1]
    first = lax.axis_index("sec") * sec_dev
    targets = first + jnp.arange(sec_dev, dtype=jnp.int32)
    rows_here = lax.dynamic_slice_in_dim(sec_rows, first, sec_dev)
    line = jnp.arange(block_rows, dtype=jnp.int32)
    kept = jnp.where((line[None, :] < rows_here[:, None])[:, :, None], psi, jnp.zeros_like(psi))
    spread = lax.all_to_all(comp_ops, "pair", split_axis=2, concat_axis=0, tiled=True)
    mirrored = lax.all_to_all(spread[::-1], "pair", split_axis=0, concat_axis=2, tiled=True)
    half = jnp.einsum(
        "psab,sbc->psac", normal_ops, kept, preferred_element_type=jnp.float32
    ).astype(jnp.bfloat16)
    terms = jnp.einsum("psac,psdc->sad", half, mirrored, preferred_element_type=jnp.float32)
    share = block_rows // lax.axis_size("pair")
    row_start = lax.axis_index("pair") * share
    partial_rows = lax.psum_scatter(terms, "pair", scatter_dimension=1, tiled=True).astype(
        jnp.bfloat16
    )
    gathered = lax.all_gather(partial_rows, "sec", axis=0, tiled=True)
    summed = pick_sources(gathered, match, targets)
    target_rows = lax.dynamic_slice_in_dim(sec_rows, first, sec_dev)
    my_lines = row_start + jnp.arange(share, dtype=jnp.int32)
    out_keep = my_lines[None, :] < target_rows[:, None]
    return jnp.where(out_keep[:, :, None], summed, jnp.zeros_like(summed))


def solution(mesh):
    in_specs = (
        P("sec", None, None),
        P(),
        P(),
        P("pair", "sec", None, None),
        P("pair", "sec", None, None),
    )
    out_specs = P("sec", "pair", None)
    return jax.shard_map(shards, mesh=mesh, in_specs=in_specs, out_specs=out_specs, check_vma=False)
```

profile of v0, /device:TPU:0, one launch (start us, length us, event | category | flops | bytes accessed | tf_op | source)
XLA Modules:
  0.0 343.5 jit_solution(5131084377381535837)
XLA Ops:
  6.5 3.0 copy.14
  9.6 60.9 %all_to_all.33 = bf16[1,8,384,384]{3,1,0,2:T(8,128)(2,1)S(1)} all-to-all(bf16[1,8,384,384]{3,1,0,2:T(8,128)(2,1)S(1)} %copy.14), channel_id=1, replica_groups=mesh['pair'=8,'sec'=4] {'pair'}, dimensions={2} | all-to-all | bytes 4718592 | tf_op jit(solution)/shard_map/all_to_all | solution.py:22
  70.5 0.3 copy.21
  70.9 0.0 copy-start
  70.9 1.7 rev.3
  72.5 3.6 %all-to-all-start.1 = ((bf16[8,8,48,384]{3,2,1,0:T(8,128)(2,1)}), bf16[8,8,48,384]{3,2,1,0:T(8,128)(2,1)S(1)}, u32[]{:S(2)}, u32[]{:S(2)}) async-start(bf16[8,8,48,384]{3,2,1,0:T(8,128)(2,1)} %rev.3), calls=%async_computation.1 | async-start | bytes 4718592 | tf_op jit(solution)/shard_map/all_to_all | solution.py:23
  76.2 0.0 reduce-scatter.2.cloned.1.call-start
  76.2 0.0 copy-done
  76.2 0.1 dynamic_slice.4
  76.3 0.1 iota_compare_fusion
  76.4 53.2 %all-to-all-done.1 = bf16[8,8,48,384]{3,2,1,0:T(8,128)(2,1)S(1)} async-done(((bf16[8,8,48,384]{3,2,1,0:T(8,128)(2,1)}), bf16[8,8,48,384]{3,2,1,0:T(8,128)(2,1)S(1)}, u32[]{:S(2)}, u32[]{:S(2)}) %all-to-all-start.1) | async-done | bytes 2359328 | tf_op jit(solution)/shard_map/all_to_all | solution.py:23
  129.6 1.6 copy.16
  131.3 13.8 %fusion.2 = f32[8,768,384]{2,1,0:T(8,128)} fusion(bf16[8,384,384]{2,1,0:T(8,128)(2,1)} %bitcast.32, bf16[1,8,768,768]{3,2,1,0:T(8,128)(2,1)} %param.8, bf16[8,768,384]{2,1,0:T(8,128)(2,1)} %param.5, pred[8,768]{1,0:T(8,128)(4,1)S(1)} %iota_compare_fusion), kind=kOutput, calls=%fused_computation.3 | convolution fusion | flops 5440536576 | bytes 25958400 | tf_op jit(solution)/shard_map/psac,psdc->sad/dot_general | solution.py:27
  145.1 0.0 copy-start.1
  145.1 0.0 reduce-scatter.2.cloned.1.call-update
  145.1 0.0 all-gather.2.cloned.1.call-start
  145.2 162.6 %reduce-scatter.2.cloned.1.call-done = f32[8,96,384]{2,1,0:T(8,128)} async-done(((f32[8,768,384]{2,1,0:T(8,128)}), f32[8,96,384]{2,1,0:T(8,128)}) %reduce-scatter.2.cloned.1.call-update) | async-done | bytes 1179664 | tf_op jit(solution)/shard_map/reduce_scatter | solution.py:30
  307.8 2.1 convert_element_type.15
  309.9 0.0 all-gather.2.cloned.1.call-update
  310.0 0.0 copy-done.1
  310.0 0.2 select_reduce_fusion
  310.2 0.1 broadcast_compare_fusion
  310.3 23.0 %all-gather.2.cloned.1.call-done = bf16[32,96,384]{2,1,0:T(8,128)(2,1)} async-done(((bf16[8,96,384]{2,1,0:T(8,128)(2,1)}), bf16[32,96,384]{2,1,0:T(8,128)(2,1)}) %all-gather.2.cloned.1.call-update) | async-done | bytes 2359312 | tf_op jit(solution)/shard_map/all_gather | solution.py:33
  333.3 2.3 gather_fusion
  335.6 1.0 broadcast_select_fusion
  (4 shorter events, 0.0 us)
Async XLA Ops:
  70.9 5.4 %copy-start = (s32[32]{0:T(128)S(1)}, s32[32]{0:T(128)}, u32[]{:S(2)}) copy-start(s32[32]{0:T(128)} %param.6) | copy-start | bytes 388
  72.5 57.1 %all-to-all-start.1 = ((bf16[8,8,48,384]{3,2,1,0:T(8,128)(2,1)}), bf16[8,8,48,384]{3,2,1,0:T(8,128)(2,1)S(1)}, u32[]{:S(2)}, u32[]{:S(2)}) async-start(bf16[8,8,48,384]{3,2,1,0:T(8,128)(2,1)} %rev.3), calls=%async_computation.1 | async-start | bytes 4718592 | tf_op jit(solution)/shard_map/all_to_all | solution.py:23
  76.2 231.6 %reduce-scatter.2.cloned.1.call-start = ((), (), s32[]{:S(2)}) async-start(), calls=%async_computation.3 | async-start | bytes 10616832 | tf_op jit(solution)/shard_map/reduce_scatter | solution.py:30
  145.1 164.9 %copy-start.1 = (s32[32]{0:T(128)S(1)}, s32[32]{0:T(128)}, u32[]{:S(2)}) copy-start(s32[32]{0:T(128)} %param.7) | copy-start | bytes 388
  145.1 188.2 %all-gather.2.cloned.1.call-start = ((), (), s32[]{:S(2)}) async-start(), calls=%async_computation.4 | async-start | bytes 2949120 | tf_op jit(solution)/shard_map/all_gather | solution.py:33
Sparse Core Ops, SparseCore 0:
  145.2 162.4 reduce-scatter.1
  310.1 23.1 all-gather.1
where the time goes:
time: 344 us; the launch traced here: 343 us
  waiting for transfers between devices  239 us (69%)
  blocking collectives  60.9 us (18%)
  matrix products  13.8 us (4%)
  between operations  13.5 us (4%)
  local copies, waits for them, and re-layouts  9.13 us (3%)
  starting transfers between devices  3.7 us (1%)
  other arithmetic  3.5 us (1%)
    reduce_scatter x1, waiting for transfers between devices, shards(): lax.psum_scatter(terms, 'pair', scatter_dimension=1, tiled=True)  163 us
    all_to_all x1, blocking collectives, shards(): lax.all_to_all(comp_ops, 'pair', split_axis=2, concat_axis=0, tiled=True)  60.9 us
    all_to_all x1, waiting for transfers between devices, shards(): lax.all_to_all(spread[::-1], 'pair', split_axis=0, concat_axis=2, tiled=T...  53.2 us
    all_gather x1, waiting for transfers between devices, shards(): gathered = lax.all_gather(partial_rows, 'sec', axis=0, tiled=True)  23 us
    dot_general x1, matrix products, shards(): jnp.einsum('psac,psdc->sad', half, mirrored, preferred_element_type=jnp.f...  13.8 us
  transfers between devices with their start and end apart: 3, of which 3 were waited for; matrix products, arithmetic and copies ran while one was open for 0% of the time, Pallas kernels for 0%

commit v1 on v0

--- a/solution.py
+++ b/solution.py
@@ -1,7 +1,14 @@
+import functools
+
 import jax
 import jax.numpy as jnp
 from jax import lax
+from jax.experimental import pallas as pl
+from jax.experimental.pallas import tpu as pltpu
 from jax.sharding import PartitionSpec as P
+
+WINDOW = 2
+MESH = pl.DeviceIdType.MESH
 
 
 def pick_sources(gathered, match, targets):
@@ -38,6 +45,200 @@
     return jnp.where(out_keep[:, :, None], summed, jnp.zeros_like(summed))
 
 
+def kernel(
+    secs, rows_ref, psi_ref, norm_ref, comp_ref, out_ref,
+    psi_v, norm_v, half_v, comp_v, acc, s1, r1, s2, r2, s3, r3, s4,
+    psi_sem, norm_sem, csend, crecv, send1, recv1, send2, recv2, send3, recv3,
+    send4, recv4, local_sem,
+):
+    n = psi_ref.shape[0]
+    mb, nb = psi_ref.shape[1:]
+    share = mb // 8
+    bf16 = jnp.bfloat16
+    pair = lax.axis_index("pair")
+    sec = lax.axis_index("sec")
+    y = pair % 2
+    z = pair // 2
+    zl = z % 2
+    zh = z // 2
+    mirror = (7 - pair, sec)
+    y_peer = (z * 2 + 1 - y, sec)
+    zl_peer = ((zh * 2 + 1 - zl) * 2 + y, sec)
+    zh_peer = (((1 - zh) * 2 + zl) * 2 + y, sec)
+    sec_peers = [(pair, (sec + k) % secs) for k in range(1, secs)]
+
+    def load(s):
+        return (
+            pltpu.make_async_copy(psi_ref.at[s], psi_v.at[s], psi_sem.at[s]),
+            pltpu.make_async_copy(norm_ref.at[0, s], norm_v.at[s], norm_sem.at[s]),
+        )
+
+    def remote(src, dst, send, recv, where):
+        return pltpu.make_async_remote_copy(
+            src_ref=src, dst_ref=dst, send_sem=send, recv_sem=recv,
+            device_id=where, device_id_type=MESH,
+        )
+
+    def comp_copy(s):
+        return remote(comp_ref.at[0, s], comp_v.at[s], csend.at[s], crecv.at[s], mirror)
+
+    def copy1(s):
+        return remote(s1.at[s], r1.at[s], send1.at[s], recv1.at[s], y_peer)
+
+    def copy2(s):
+        return remote(s2.at[s], r2.at[s], send2.at[s], recv2.at[s], zl_peer)
+
+    def copy3(s):
+        return remote(s3.at[s], r3.at[s], send3.at[s], recv3.at[s], zh_peer)
+
+    def copy4(s, k):
+        return remote(
+            s4.at[s], out_ref.at[sec * n + s], send4.at[k, s], recv4.at[k, s], sec_peers[k]
+        )
+
+    def keep4(s):
+        return pltpu.make_async_copy(s4.at[s], out_ref.at[sec * n + s], local_sem.at[s])
+
+    barrier = pltpu.get_barrier_semaphore()
+    peers = [mirror, y_peer, zl_peer, zh_peer] + sec_peers
+    for peer in peers:
+        pl.semaphore_signal(barrier, inc=1, device_id=peer, device_id_type=MESH)
+    for s in range(n):
+        for c in load(s):
+            c.start()
+    pl.semaphore_wait(barrier, len(peers))
+    for s in range(WINDOW):
+        comp_copy(s).start()
+
+    @pl.loop(0, n)
+    def _(s):
+        for c in load(s):
+            c.wait()
+        line = lax.broadcasted_iota(jnp.int32, (mb, nb), 0)
+        value = psi_v[s].astype(jnp.float32)
+        kept = jnp.where(line < rows_ref[sec * n + s], value, 0.0).astype(bf16)
+        got = jnp.dot(norm_v[s], kept, preferred_element_type=jnp.float32).astype(bf16)
+        for b in range(8):
+            half_v[s, b % 2, b // 2] = got[b * share : (b + 1) * share]
+
+    def image(s, which):
+        rows = half_v[s, which].reshape(mb // 2, nb)
+        return lax.dot_general(
+            rows, comp_v[s], (((1,), (1,)), ((), ())), preferred_element_type=jnp.float32
+        )
+
+    @pl.loop(0, n + 3)
+    def _(step):
+        @pl.when(step >= 3)
+        def _():
+            s = step - 3
+            copy3(s).wait()
+            s4[s] = (acc[s, zh, zl] + r3[s].astype(jnp.float32)).astype(bf16)
+            keep4(s).start()
+            for k in range(secs - 1):
+                copy4(s, k).start()
+
+        @pl.when((step >= 2) & (step < n + 2))
+        def _():
+            s = step - 2
+            copy2(s).wait()
+            s3[s] = (acc[s, 1 - zh, zl] + r2[s, 1 - zh].astype(jnp.float32)).astype(bf16)
+            copy3(s).start()
+            acc[s, zh, zl] = acc[s, zh, zl] + r2[s, zh].astype(jnp.float32)
+
+        @pl.when((step >= 1) & (step < n + 1))
+        def _():
+            s = step - 1
+            copy1(s).wait()
+            for h in range(2):
+                s2[s, h] = (acc[s, h, 1 - zl] + r1[s, h, 1 - zl].astype(jnp.float32)).astype(bf16)
+            copy2(s).start()
+            for h in range(2):
+                acc[s, h, zl] = acc[s, h, zl] + r1[s, h, zl].astype(jnp.float32)
+
+        @pl.when(step < n)
+        def _():
+            s = step
+            comp_copy(s).wait()
+
+            @pl.when(s + WINDOW < n)
+            def _():
+                comp_copy(s + WINDOW).start()
+
+            s1[s] = image(s, 1 - y).astype(bf16).reshape(2, 2, share, nb)
+            copy1(s).start()
+            acc[s] = image(s, y).reshape(2, 2, share, nb)
+
+    @pl.loop(0, n)
+    def _(s):
+        keep4(s).wait()
+        for k in range(secs - 1):
+            copy4(s, k).wait()
+
+
+def place_kernel(source_ref, rows_ref, start_ref, in_ref, out_ref):
+    t = pl.program_id(0)
+    share, nb = out_ref.shape[1:]
+    line = start_ref[0] + lax.broadcasted_iota(jnp.int32, (share, nb), 0)
+    value = in_ref[0].astype(jnp.float32)
+    out_ref[0] = jnp.where(line < rows_ref[t], value, 0.0).astype(out_ref.dtype)
+
+
+def kernel_shards(secs, psi, sec_rows, match, normal_ops, comp_ops):
+    n, mb, nb = psi.shape
+    total = match.shape[0]
+    share = mb // 8
+    bf16 = jnp.bfloat16
+    vmem = pltpu.VMEM
+    dma = pltpu.SemaphoreType.DMA
+    gathered = pl.pallas_call(
+        functools.partial(kernel, secs),
+        out_shape=jax.ShapeDtypeStruct((total, share, nb), bf16),
+        in_specs=[pl.BlockSpec(memory_space=pltpu.SMEM)] + [pl.BlockSpec(memory_space=pl.ANY)] * 3,
+        out_specs=pl.BlockSpec(memory_space=pl.ANY),
+        scratch_shapes=[
+            vmem((n, mb, nb), bf16),
+            vmem((n, mb, mb), bf16),
+            vmem((n, 2, 4, share, nb), bf16),
+            vmem((n, nb, nb), bf16),
+            vmem((n, 2, 2, share, nb), jnp.float32),
+            vmem((n, 2, 2, share, nb), bf16),
+            vmem((n, 2, 2, share, nb), bf16),
+            vmem((n, 2, share, nb), bf16),
+            vmem((n, 2, share, nb), bf16),
+            vmem((n, share, nb), bf16),
+            vmem((n, share, nb), bf16),
+            vmem((n, share, nb), bf16),
+        ]
+        + [dma((n,))] * 10
+        + [dma((secs - 1, n))] * 2
+        + [dma((n,))],
+        compiler_params=pltpu.CompilerParams(
+            collective_id=0, has_side_effects=True, vmem_limit_bytes=56 * 1024 * 1024
+        ),
+        cost_estimate=pl.CostEstimate(
+            flops=2 * n * mb * nb * (mb + nb), bytes_accessed=20_000_000, transcendentals=0
+        ),
+    )(sec_rows, psi, normal_ops, comp_ops)
+
+    first = lax.axis_index("sec") * n
+    targets = first + jnp.arange(n, dtype=jnp.int32)
+    hits = match[None, :] == targets[:, None]
+    source = jnp.sum(jnp.where(hits, jnp.arange(total, dtype=jnp.int32)[None, :], 0), axis=1)
+    target_rows = lax.dynamic_slice_in_dim(sec_rows, first, n)
+    start = (lax.axis_index("pair") * share).astype(jnp.int32)[None]
+    return pl.pallas_call(
+        place_kernel,
+        out_shape=jax.ShapeDtypeStruct((n, share, nb), bf16),
+        grid_spec=pltpu.PrefetchScalarGridSpec(
+            num_scalar_prefetch=3,
+            grid=(n,),
+            in_specs=[pl.BlockSpec((1, share, nb), lambda t, src, rows, st: (src[t], 0, 0))],
+            out_specs=pl.BlockSpec((1, share, nb), lambda t, src, rows, st: (t, 0, 0)),
+        ),
+    )(source, target_rows, start, gathered)
+
+
 def solution(mesh):
     in_specs = (
         P("sec", None, None),
@@ -47,4 +248,7 @@
         P("pair", "sec", None, None),
     )
     out_specs = P("sec", "pair", None)
-    return jax.shard_map(shards, mesh=mesh, in_specs=in_specs, out_specs=out_specs, check_vma=False)
+    body = shards
+    if mesh.shape["pair"] == 8:
+        body = functools.partial(kernel_shards, mesh.shape["sec"])
+    return jax.shard_map(body, mesh=mesh, in_specs=in_specs, out_specs=out_specs, check_vma=False)

time: 344 us -> 158 us (0.46)
  waiting for transfers between devices: 239 us -> 0 us
  Pallas kernels: 0 us -> 154 us
  blocking collectives: 60.9 us -> 0 us
  matrix products: 13.8 us -> 0 us
  between operations: 13.5 us -> 0.01 us
  local copies, waits for them, and re-layouts: 9.13 us -> 1.25 us
  starting transfers between devices: 3.7 us -> 0 us
    reduce_scatter x1 -> x0, waiting for transfers between devices: 163 us -> none  [shards(): lax.psum_scatter(terms, 'pair', scatter_dimension=1, tiled=True)]
    pallas_call x0 -> x2, Pallas kernels: none -> 154 us  [the longest x1 148 us: kernel_shards(): pl.pallas_call(functools.partial(kernel, secs), out_shape=jax.ShapeDtypeS...]
    all_to_all x1 -> x0, blocking collectives: 60.9 us -> none  [shards(): lax.all_to_all(comp_ops, 'pair', split_axis=2, concat_axis=0, tiled=True)]
    all_to_all x1 -> x0, waiting for transfers between devices: 53.2 us -> none  [shards(): lax.all_to_all(spread[::-1], 'pair', split_axis=0, concat_axis=2, tiled=T...]
    all_gather x1 -> x0, waiting for transfers between devices: 23 us -> none  [shards(): gathered = lax.all_gather(partial_rows, 'sec', axis=0, tiled=True)]
    dot_general x1 -> x0, matrix products: 13.8 us -> none  [shards(): jnp.einsum('psac,psdc->sad', half, mirrored, preferred_element_type=jnp.f...]
    all_to_all x1 -> x0, starting transfers between devices: 3.61 us -> none  [shards(): lax.all_to_all(spread[::-1], 'pair', split_axis=0, concat_axis=2, tiled=T...]
  transfers between devices with their start and end apart: 3 -> 0, of which waited for: 3 -> 0; matrix products, arithmetic and copies ran while one was open for 0% -> 0% of each run, Pallas kernels for 0% -> 0%
where the time goes in v1:
time: 158 us; the launch traced here: 156 us
  Pallas kernels  154 us (97%)
    pallas_call x1, Pallas kernels, kernel_shards(): pl.pallas_call(functools.partial(kernel, secs), out_shape=jax.ShapeDtypeS...  148 us
    pallas_call x1, Pallas kernels, kernel_shards(): pl.pallas_call(place_kernel, out_shape=jax.ShapeDtypeStruct((n, share, nb...  5.7 us

profile of v1, /device:TPU:0, one launch (start us, length us, event | category | flops | bytes accessed | tf_op | source)
XLA Modules:
  0.0 156.5 jit_solution(5985178501696005)
XLA Ops:
  0.0 1.2 dynamic_slice.3.rows_ref
  1.3 1.3 select_reduce_fusion.source_ref
  2.6 148.2 %shard_map.55.in_ref = bf16[32,96,384]{2,1,0:T(8,128)(2,1)} custom-call(s32[32]{0:T(128)} %rows_ref.1, bf16[8,768,384]{2,1,0:T(8,128)(2,1)} %psi_ref.1, bf16[1,8,768,768]{3,2,1,0:T(8,128)(2,1)} %norm_ref.1, bf16[1,8,384,384]{3,2,1,0:T(8,128)(2,1)} %comp_ref.1), custom_call_target="tpu_custom_call" | custom-call | flops 5435817984 | bytes 20000000 | tf_op jit(solution)/shard_map/pallas_call | solution.py:194
  150.8 5.7 %shard_map.56 = bf16[8,96,384]{2,1,0:T(8,128)(2,1)} custom-call(s32[8]{0:T(128)} %select_reduce_fusion.source_ref, s32[8]{0:T(128)} %dynamic_slice.3.rows_ref, s32[1]{0:T(128)} %bitcast.start_ref, bf16[32,96,384]{2,1,0:T(8,128)(2,1)} %shard_map.55.in_ref), custom_call_target="tpu_custom_call" | custom-call | tf_op jit(solution)/shard_map/pallas_call | solution.py:230
  (1 shorter events, 0.0 us)

commit v2 on v1

v2 whole, which is shorter than its diff:
```python
import functools

import jax
import jax.numpy as jnp
from jax import lax
from jax.experimental import pallas as pl
from jax.experimental.pallas import tpu as pltpu
from jax.sharding import PartitionSpec as P

WINDOW = 4
LAGS = (3, 6, 9)
LANES = 128
MESH = pl.DeviceIdType.MESH


def pick_sources(gathered, match, targets):
    total = match.shape[0]
    hits = match[None, :] == targets[:, None]
    source = jnp.sum(jnp.where(hits, jnp.arange(total, dtype=jnp.int32)[None, :], 0), axis=1)
    return gathered[source]


def shards(psi, sec_rows, match, normal_ops, comp_ops):
    sec_dev = psi.shape[0]
    block_rows = psi.shape[1]
    first = lax.axis_index("sec") * sec_dev
    targets = first + jnp.arange(sec_dev, dtype=jnp.int32)
    rows_here = lax.dynamic_slice_in_dim(sec_rows, first, sec_dev)
    line = jnp.arange(block_rows, dtype=jnp.int32)
    kept = jnp.where((line[None, :] < rows_here[:, None])[:, :, None], psi, jnp.zeros_like(psi))
    spread = lax.all_to_all(comp_ops, "pair", split_axis=2, concat_axis=0, tiled=True)
    mirrored = lax.all_to_all(spread[::-1], "pair", split_axis=0, concat_axis=2, tiled=True)
    half = jnp.einsum(
        "psab,sbc->psac", normal_ops, kept, preferred_element_type=jnp.float32
    ).astype(jnp.bfloat16)
    terms = jnp.einsum("psac,psdc->sad", half, mirrored, preferred_element_type=jnp.float32)
    share = block_rows // lax.axis_size("pair")
    row_start = lax.axis_index("pair") * share
    partial_rows = lax.psum_scatter(terms, "pair", scatter_dimension=1, tiled=True).astype(
        jnp.bfloat16
    )
    gathered = lax.all_gather(partial_rows, "sec", axis=0, tiled=True)
    summed = pick_sources(gathered, match, targets)
    target_rows = lax.dynamic_slice_in_dim(sec_rows, first, sec_dev)
    my_lines = row_start + jnp.arange(share, dtype=jnp.int32)
    out_keep = my_lines[None, :] < target_rows[:, None]
    return jnp.where(out_keep[:, :, None], summed, jnp.zeros_like(summed))


def kernel(
    secs, rows_ref, psi_ref, norm_ref, comp_ref, out_ref,
    psi_v, norm_v, half_v, comp_v, acc, s1, r1, s2, r2, s3, r3, s4,
    psi_sem, norm_sem, csend, crecv, send1, recv1, send2, recv2, send3, recv3,
    send4, recv4, local_sem,
):
    n = psi_ref.shape[0]
    mb, nb = psi_ref.shape[1:]
    cuts = nb // LANES
    pieces = n * cuts
    share = mb // 8
    lag2, lag3, lag4 = LAGS
    bf16 = jnp.bfloat16
    f32 = jnp.float32
    pair = lax.axis_index("pair")
    sec = lax.axis_index("sec")
    y = pair % 2
    z = pair // 2
    zl = z % 2
    zh = z // 2
    mirror = (7 - pair, sec)
    y_peer = (z * 2 + 1 - y, sec)
    zl_peer = ((zh * 2 + 1 - zl) * 2 + y, sec)
    zh_peer = (((1 - zh) * 2 + zl) * 2 + y, sec)
    sec_peers = [(pair, (sec + k) % secs) for k in range(1, secs)]

    def load(s):
        return (
            pltpu.make_async_copy(psi_ref.at[s], psi_v.at[s], psi_sem.at[s]),
            pltpu.make_async_copy(norm_ref.at[0, s], norm_v.at[s], norm_sem.at[s]),
        )

    def remote(src, dst, send, recv, where):
        return pltpu.make_async_remote_copy(
            src_ref=src, dst_ref=dst, send_sem=send, recv_sem=recv,
            device_id=where, device_id_type=MESH,
        )

    def comp_copy(j):
        lines = pl.ds(pl.multiple_of((j % cuts) * LANES, LANES), LANES)
        return remote(
            comp_ref.at[0, j // cuts, lines], comp_v.at[j], csend.at[j], crecv.at[j], mirror
        )

    def copy1(j):
        return remote(s1.at[j], r1.at[j], send1.at[j], recv1.at[j], y_peer)

    def copy2(j):
        return remote(s2.at[j], r2.at[j], send2.at[j], recv2.at[j], zl_peer)

    def copy3(j):
        return remote(s3.at[j], r3.at[j], send3.at[j], recv3.at[j], zh_peer)

    def copy4(j, k):
        return remote(
            s4.at[j], out_ref.at[sec * pieces + j], send4.at[k, j], recv4.at[k, j], sec_peers[k]
        )

    def keep4(j):
        return pltpu.make_async_copy(s4.at[j], out_ref.at[sec * pieces + j], local_sem.at[j])

    barrier = pltpu.get_barrier_semaphore()
    peers = [mirror, y_peer, zl_peer, zh_peer] + sec_peers
    for peer in peers:
        pl.semaphore_signal(barrier, inc=1, device_id=peer, device_id_type=MESH)
    for s in range(n):
        for c in load(s):
            c.start()
    pl.semaphore_wait(barrier, len(peers))
    for j in range(WINDOW):
        comp_copy(j).start()

    def make_half(s):
        for c in load(s):
            c.wait()
        line = lax.broadcasted_iota(jnp.int32, (mb, nb), 0)
        kept = jnp.where(line < rows_ref[sec * n + s], psi_v[s].astype(f32), 0.0).astype(bf16)
        got = jnp.dot(norm_v[s], kept, preferred_element_type=f32).astype(bf16)
        for b in range(8):
            half_v[s, b % 2, b // 2] = got[b * share : (b + 1) * share]

    make_half(0)

    def image(j, which):
        rows = half_v[j // cuts, which].reshape(mb // 2, nb)
        got = lax.dot_general(
            rows, comp_v[j], (((1,), (1,)), ((), ())), preferred_element_type=f32
        )
        return got.reshape(2, 2, share, LANES)

    @pl.loop(0, pieces + lag4)
    def _(step):
        @pl.when(step >= lag4)
        def _():
            j = step - lag4
            copy3(j).wait()
            s4[j] = (acc[j, zh, zl] + r3[j].astype(f32)).astype(bf16)
            keep4(j).start()
            for k in range(secs - 1):
                copy4(j, k).start()

        @pl.when((step >= lag3) & (step < pieces + lag3))
        def _():
            j = step - lag3
            copy2(j).wait()
            s3[j] = (acc[j, 1 - zh, zl] + r2[j, 1 - zh].astype(f32)).astype(bf16)
            copy3(j).start()
            acc[j, zh, zl] = acc[j, zh, zl] + r2[j, zh].astype(f32)

        @pl.when((step >= lag2) & (step < pieces + lag2))
        def _():
            j = step - lag2
            copy1(j).wait()
            for h in range(2):
                s2[j, h] = (acc[j, h, 1 - zl] + r1[j, h, 1 - zl].astype(f32)).astype(bf16)
            copy2(j).start()
            for h in range(2):
                acc[j, h, zl] = acc[j, h, zl] + r1[j, h, zl].astype(f32)

        @pl.when(step < pieces)
        def _():
            j = step
            comp_copy(j).wait()

            @pl.when(j + WINDOW < pieces)
            def _():
                comp_copy(j + WINDOW).start()

            s1[j] = image(j, 1 - y).astype(bf16)
            copy1(j).start()
            acc[j] = image(j, y)

            @pl.when((j % cuts == 0) & (j + cuts < pieces))
            def _():
                make_half(j // cuts + 1)

    @pl.loop(0, pieces)
    def _(j):
        keep4(j).wait()
        for k in range(secs - 1):
            copy4(j, k).wait()


def place_kernel(rows_ref, match_ref, in_ref, out_ref, source):
    n, share, nb = out_ref.shape
    first = lax.axis_index("sec") * n
    start = lax.axis_index("pair") * share
    cuts = nb // LANES

    for i in range(match_ref.shape[0]):
        t = match_ref[i] - first

        @pl.when((t >= 0) & (t < n))
        def _():
            source[t] = i

    @pl.loop(0, n)
    def _(t):
        line = start + lax.broadcasted_iota(jnp.int32, (share, LANES), 0)
        keep = line < rows_ref[first + t]
        for c in range(cuts):
            value = in_ref[source[t] * cuts + c].astype(jnp.float32)
            value = jnp.where(keep, value, 0.0).astype(out_ref.dtype)
            out_ref[t, :, c * LANES : (c + 1) * LANES] = value


def kernel_shards(secs, psi, sec_rows, match, normal_ops, comp_ops):
    n, mb, nb = psi.shape
    share = mb // 8
    pieces = n * (nb // LANES)
    bf16 = jnp.bfloat16
    vmem = pltpu.VMEM
    dma = pltpu.SemaphoreType.DMA
    gathered = pl.pallas_call(
        functools.partial(kernel, secs),
        out_shape=jax.ShapeDtypeStruct((secs * pieces, share, LANES), bf16),
        in_specs=[pl.BlockSpec(memory_space=pltpu.SMEM)] + [pl.BlockSpec(memory_space=pl.ANY)] * 3,
        out_specs=pl.BlockSpec(memory_space=pl.ANY),
        scratch_shapes=[
            vmem((n, mb, nb), bf16),
            vmem((n, mb, mb), bf16),
            vmem((n, 2, 4, share, nb), bf16),
            vmem((pieces, LANES, nb), bf16),
            vmem((pieces, 2, 2, share, LANES), jnp.float32),
            vmem((pieces, 2, 2, share, LANES), bf16),
            vmem((pieces, 2, 2, share, LANES), bf16),
            vmem((pieces, 2, share, LANES), bf16),
            vmem((pieces, 2, share, LANES), bf16),
            vmem((pieces, share, LANES), bf16),
            vmem((pieces, share, LANES), bf16),
            vmem((pieces, share, LANES), bf16),
        ]
        + [dma((n,))] * 2
        + [dma((pieces,))] * 8
        + [dma((secs - 1, pieces))] * 2
        + [dma((pieces,))],
        compiler_params=pltpu.CompilerParams(
            collective_id=0, has_side_effects=True, vmem_limit_bytes=56 * 1024 * 1024
        ),
        cost_estimate=pl.CostEstimate(
            flops=2 * n * mb * nb * (mb + nb), bytes_accessed=20_000_000, transcendentals=0
        ),
    )(sec_rows, psi, normal_ops, comp_ops)
    return pl.pallas_call(
        place_kernel,
        out_shape=jax.ShapeDtypeStruct((n, share, nb), bf16),
        in_specs=[pl.BlockSpec(memory_space=pltpu.SMEM)] * 2
        + [pl.BlockSpec(memory_space=pltpu.VMEM)],
        out_specs=pl.BlockSpec(memory_space=pltpu.VMEM),
        scratch_shapes=[pltpu.SMEM((n,), jnp.int32)],
        compiler_params=pltpu.CompilerParams(vmem_limit_bytes=16 * 1024 * 1024),
    )(sec_rows, match, gathered)


def solution(mesh):
    in_specs = (
        P("sec", None, None),
        P(),
        P(),
        P("pair", "sec", None, None),
        P("pair", "sec", None, None),
    )
    out_specs = P("sec", "pair", None)
    body = shards
    if mesh.shape["pair"] == 8:
        body = functools.partial(kernel_shards, mesh.shape["sec"])
    return jax.shard_map(body, mesh=mesh, in_specs=in_specs, out_specs=out_specs, check_vma=False)
```

time: 158 us -> 148 us (0.937)
  Pallas kernels: 154 us -> 146 us
    pallas_call x1, Pallas kernels: 5.7 us -> 1.62 us  [kernel_shards(): pl.pallas_call(place_kernel, out_shape=jax.ShapeDtypeStruct((n, share, nb...]
    pallas_call x1, Pallas kernels: 148 us -> 144 us  [kernel_shards(): pl.pallas_call(functools.partial(kernel, secs), out_shape=jax.ShapeDtypeS...]
    unnamed x0 -> x6, local copies, waits for them, and re-layouts: none -> 1.67 us
where the time goes in v2:
time: 148 us
  Pallas kernels  146 us (99%)
  local copies, waits for them, and re-layouts  1.67 us (1%)
    pallas_call x1, Pallas kernels, kernel_shards(): pl.pallas_call(functools.partial(kernel, secs), out_shape=jax.ShapeDtypeS...  144 us

profile of v2, /device:TPU:0, one launch (start us, length us, event | category | flops | bytes accessed | tf_op | source)
XLA Modules:
  0.0 147.7 jit_solution(15561108711799651771)
XLA Ops:
  0.0 0.0 copy-start.1
  0.0 0.0 copy-start.2
  0.0 144.4 %shard_map.55.in_ref = bf16[96,96,128]{2,1,0:T(8,128)(2,1)} custom-call(s32[32]{0:T(128)} %rows_ref.3, bf16[8,768,384]{2,1,0:T(8,128)(2,1)} %psi_ref.1, bf16[1,8,768,768]{3,2,1,0:T(8,128)(2,1)} %norm_ref.1, bf16[1,8,384,384]{3,2,1,0:T(8,128)(2,1)} %comp_ref.1), custom_call_target="tpu_custom_call" | custom-call | flops 5435817984 | bytes 20000000 | tf_op jit(solution)/shard_map/pallas_call | solution.py:223
  144.4 0.0 copy-done.1
  144.4 0.0 copy-done.2
  144.4 0.0 copy-start
  144.4 1.7 %copy-done = bf16[96,96,128]{2,1,0:T(8,128)(2,1)S(1)} copy-done((bf16[96,96,128]{2,1,0:T(8,128)(2,1)S(1)}, bf16[96,96,128]{2,1,0:T(8,128)(2,1)}, u32[]{:S(2)}) %copy-start) | copy-done | bytes 2359320
  146.1 1.6 %shard_map.56 = bf16[8,96,384]{2,1,0:T(8,128)(2,1)} custom-call(s32[32]{0:T(128)S(1)} %copy-done.1, s32[32]{0:T(128)S(1)} %copy-done.2, bf16[96,96,128]{2,1,0:T(8,128)(2,1)S(1)} %copy-done), custom_call_target="tpu_custom_call" | custom-call | tf_op jit(solution)/shard_map/pallas_call | solution.py:253
Async XLA Ops:
  0.0 144.4 %copy-start.1 = (s32[32]{0:T(128)S(1)}, s32[32]{0:T(128)}, u32[]{:S(2)}) copy-start(s32[32]{0:T(128)} %rows_ref.3) | copy-start | bytes 388
  0.0 144.4 %copy-start.2 = (s32[32]{0:T(128)S(1)}, s32[32]{0:T(128)}, u32[]{:S(2)}) copy-start(s32[32]{0:T(128)} %match_ref.1) | copy-start | bytes 388
  144.4 1.7 %copy-start = (bf16[96,96,128]{2,1,0:T(8,128)(2,1)S(1)}, bf16[96,96,128]{2,1,0:T(8,128)(2,1)}, u32[]{:S(2)}) copy-start(bf16[96,96,128]{2,1,0:T(8,128)(2,1)} %shard_map.55.in_ref) | copy-start | bytes 7077892

commit v3 on v2

--- a/solution.py
+++ b/solution.py
@@ -8,7 +8,7 @@
 from jax.sharding import PartitionSpec as P
 
 WINDOW = 4
-LAGS = (3, 6, 9)
+LAGS = (4, 8, 12)
 LANES = 128
 MESH = pl.DeviceIdType.MESH
 
@@ -139,6 +139,23 @@
 
     @pl.loop(0, pieces + lag4)
     def _(step):
+        @pl.when(step < pieces)
+        def _():
+            j = step
+            comp_copy(j).wait()
+
+            @pl.when(j + WINDOW < pieces)
+            def _():
+                comp_copy(j + WINDOW).start()
+
+            s1[j] = image(j, 1 - y).astype(bf16)
+            copy1(j).start()
+            acc[j] = image(j, y)
+
+            @pl.when((j % cuts == 0) & (j + cuts < pieces))
+            def _():
+                make_half(j // cuts + 1)
+
         @pl.when(step >= lag4)
         def _():
             j = step - lag4
@@ -165,23 +182,6 @@
             copy2(j).start()
             for h in range(2):
                 acc[j, h, zl] = acc[j, h, zl] + r1[j, h, zl].astype(f32)
-
-        @pl.when(step < pieces)
-        def _():
-            j = step
-            comp_copy(j).wait()
-
-            @pl.when(j + WINDOW < pieces)
-            def _():
-                comp_copy(j + WINDOW).start()
-
-            s1[j] = image(j, 1 - y).astype(bf16)
-            copy1(j).start()
-            acc[j] = image(j, y)
-
-            @pl.when((j % cuts == 0) & (j + cuts < pieces))
-            def _():
-                make_half(j // cuts + 1)
 
     @pl.loop(0, pieces)
     def _(j):

time: 148 us -> 148 us (level)
  no operation moved by 1% of the time
where the time goes in v3:
time: 148 us; the launch traced here: 147 us
  Pallas kernels  146 us (99%)
  local copies, waits for them, and re-layouts  1.67 us (1%)
    pallas_call x1, Pallas kernels, kernel_shards(): pl.pallas_call(functools.partial(kernel, secs), out_shape=jax.ShapeDtypeS...  144 us

profile of v3, /device:TPU:0, one launch (start us, length us, event | category | flops | bytes accessed | tf_op | source)
XLA Modules:
  0.0 147.4 jit_solution(10812066914849633692)
XLA Ops:
  0.0 0.0 copy-start.1
  0.0 0.0 copy-start.2
  0.0 144.1 %shard_map.55.in_ref = bf16[96,96,128]{2,1,0:T(8,128)(2,1)} custom-call(s32[32]{0:T(128)} %rows_ref.3, bf16[8,768,384]{2,1,0:T(8,128)(2,1)} %psi_ref.1, bf16[1,8,768,768]{3,2,1,0:T(8,128)(2,1)} %norm_ref.1, bf16[1,8,384,384]{3,2,1,0:T(8,128)(2,1)} %comp_ref.1), custom_call_target="tpu_custom_call" | custom-call | flops 5435817984 | bytes 20000000 | tf_op jit(solution)/shard_map/pallas_call | solution.py:223
  144.1 0.0 copy-done.1
  144.1 0.0 copy-done.2
  144.1 0.0 copy-start
  144.1 1.7 %copy-done = bf16[96,96,128]{2,1,0:T(8,128)(2,1)S(1)} copy-done((bf16[96,96,128]{2,1,0:T(8,128)(2,1)S(1)}, bf16[96,96,128]{2,1,0:T(8,128)(2,1)}, u32[]{:S(2)}) %copy-start) | copy-done | bytes 2359320
  145.8 1.6 %shard_map.56 = bf16[8,96,384]{2,1,0:T(8,128)(2,1)} custom-call(s32[32]{0:T(128)S(1)} %copy-done.1, s32[32]{0:T(128)S(1)} %copy-done.2, bf16[96,96,128]{2,1,0:T(8,128)(2,1)S(1)} %copy-done), custom_call_target="tpu_custom_call" | custom-call | tf_op jit(solution)/shard_map/pallas_call | solution.py:253
Async XLA Ops:
  0.0 144.1 %copy-start.1 = (s32[32]{0:T(128)S(1)}, s32[32]{0:T(128)}, u32[]{:S(2)}) copy-start(s32[32]{0:T(128)} %rows_ref.3) | copy-start | bytes 388
  0.0 144.1 %copy-start.2 = (s32[32]{0:T(128)S(1)}, s32[32]{0:T(128)}, u32[]{:S(2)}) copy-start(s32[32]{0:T(128)} %match_ref.1) | copy-start | bytes 388
  144.1 1.7 %copy-start = (bf16[96,96,128]{2,1,0:T(8,128)(2,1)S(1)}, bf16[96,96,128]{2,1,0:T(8,128)(2,1)}, u32[]{:S(2)}) copy-start(bf16[96,96,128]{2,1,0:T(8,128)(2,1)} %shard_map.55.in_ref) | copy-start | bytes 7077892
